TPU v7x, 32 devices: a whole 2x2x4 slice. The times are simulated.
32 devices in a mesh: wide: 8 (over z, x), narrow: 4 (over y, core).
Axes of the slice: x: 2, y: 2, z: 4, core: 2. Of those that a mesh axis runs over, the one named last changes fastest.
Arguments:
- amplitudes: float32 [240, 72000], P('narrow', 'wide'), may hold values from -6 to 6
- integrals: float32 [72000, 1920], P('wide', 'narrow'), may hold values from -0.0234375 to 0.0234375
- occupied_energy: float32 [60], replicated, may hold values from -3 to -1
- virtual_energy_rows: float32 [4], replicated, may hold values from 0.2 to 1.2
- virtual_energy_cols: float32 [32], replicated, may hold values from 0.2 to 1.2
Outputs:
- amplitude_step: float32 [240, 1920], P('wide', 'narrow')
All inputs are finite; a program needn't handle non-finite values.
Results may differ from a plain program's by a relative error of at most 0.00012.
Values sent between devices are 32-bit elements; how exact they have to be, the bound alone decides.
A program may use at most 64 MiB of HBM per device.

v0:
```python
import functools

import jax
import jax.numpy as jnp
from jax import lax
from jax.experimental import pallas as pl
from jax.experimental.pallas import tpu as pltpu
from jax.sharding import PartitionSpec as P

MESH = pl.DeviceIdType.MESH
F32 = jnp.float32
BF16 = jnp.bfloat16
DEPTH = 1152
BLOCK = 80


def halves(values):
    high = values.astype(BF16)
    return high, (values - high.astype(F32)).astype(BF16)


def by_rows(left, right):
    return lax.dot_general(
        left, right, (((1,), (1,)), ((), ())), preferred_element_type=F32
    )


def cycle_kernel(
    wides, amp, ints, out,
    own, mine, twin, far, far_twin, wide_ints, ints_high, ints_low,
    even, odd, group_sum, last_even, last_odd,
    send_big, send_small, recv_big, recv_small,
    own_sem, ints_sem, far_send, far_recv, pass_send, pass_recv, twin_send, twin_recv,
    sum_send, sum_recv,
):
    rows, pairs = amp.shape
    owner_rows = rows // 2
    third = 2 * owner_rows // 5
    small = owner_rows - 2 * third
    steps = mine.shape[0]
    slices = ints_high.shape[0]
    me = lax.axis_index("wide")
    narrow = lax.axis_index("narrow")
    across = lax.div(narrow, 2)
    core = lax.rem(narrow, 2)
    sibling = narrow + 1 - 2 * core
    neighbour = narrow + 2 - 4 * across
    diagonal = sibling + 2 - 4 * across
    shards = (narrow, sibling, neighbour, diagonal)

    own_copy = pltpu.make_async_copy(amp, own, own_sem)
    own_copy.start()

    def ints_copy(b):
        part = pl.ds(b * BLOCK, BLOCK)
        return pltpu.make_async_copy(ints.at[part], wide_ints.at[part], ints_sem.at[b])

    blocks = ints.shape[0] // BLOCK
    for b in range(blocks):
        ints_copy(b).start()

    barrier = pltpu.get_barrier_semaphore()
    for other in (sibling, neighbour):
        pl.semaphore_signal(barrier, inc=1, device_id=(me, other), device_id_type=MESH)
    for hop in range(1, wides):
        pl.semaphore_signal(
            barrier, inc=1, device_id=(lax.rem(me + hop, wides), narrow), device_id_type=MESH
        )
    pl.semaphore_wait(barrier, wides + 1)

    def far_copy(i):
        return pltpu.make_async_remote_copy(
            src_ref=mine.at[i], dst_ref=far.at[i],
            send_sem=far_send.at[i], recv_sem=far_recv.at[i],
            device_id=(me, neighbour), device_id_type=MESH,
        )

    def pass_copy(i):
        return pltpu.make_async_remote_copy(
            src_ref=far.at[i], dst_ref=far_twin.at[i],
            send_sem=pass_send.at[i], recv_sem=pass_recv.at[i],
            device_id=(me, sibling), device_id_type=MESH,
        )

    twin_copy = pltpu.make_async_remote_copy(
        src_ref=mine, dst_ref=twin, send_sem=twin_send, recv_sem=twin_recv,
        device_id=(me, sibling), device_id_type=MESH,
    )

    def pack(i, at, first, count, k):
        length = min(DEPTH, pairs - k * DEPTH)
        mine[i, at:at + count, :length] = own[first:first + count, k * DEPTH:k * DEPTH + length]
        if length < DEPTH:
            mine[i, at:at + count, length:] = jnp.zeros((count, DEPTH - length), F32)

    own_copy.wait()
    for g in range(2):
        for k in range(slices):
            i = g * slices + k
            pack(i, 0, g * third, third, k)
            pack(i, third, owner_rows + g * third, third, k)
            far_copy(i).start()
    for j in range(slices // 2):
        i = 2 * slices + j
        for p in range(2):
            pack(i, 2 * small * p, 2 * third, small, 2 * j + p)
            pack(i, 2 * small * p + small, owner_rows + 2 * third, small, 2 * j + p)
        far_copy(i).start()
    twin_copy.start()

    def sum_copy(s, h, g):
        owner = 2 * shards[s] + h
        src = send_big.at[s, h, g] if g < 2 else send_small.at[s, h]
        dst = recv_big.at[g, me] if g < 2 else recv_small.at[me]
        copy = pltpu.make_async_remote_copy(
            src_ref=src, dst_ref=dst,
            send_sem=sum_send.at[s, h, g], recv_sem=sum_recv.at[g, me],
            device_id=(owner, narrow), device_id_type=MESH,
        )
        return owner, copy

    def emit(s, h, g, value):
        if g < 2:
            send_big[s, h, g] = value
        else:
            send_small[s, h] = value
        owner, copy = sum_copy(s, h, g)

        @pl.when(owner == me)
        def _():
            if g < 2:
                recv_big[g, me] = value
            else:
                recv_small[me] = value

        @pl.when(owner != me)
        def _():
            copy.start()

    def product(values, k):
        high, low = halves(values)
        count = values.shape[0]
        both = by_rows(jnp.concatenate([high, low], axis=0), ints_high[k])
        rest = by_rows(high, ints_low[k])
        return both[:count] + (both[count:] + rest)

    even[...] = jnp.zeros_like(even)
    odd[...] = jnp.zeros_like(odd)

    def split_block(b, carry):
        ints_copy(b).wait()

        def split(t, inner):
            part = pl.ds(pl.multiple_of(b * BLOCK + t * 16, 16), 16)
            for k in range(slices):
                length = min(DEPTH, pairs - k * DEPTH)
                high, low = halves(wide_ints[part, k * DEPTH:k * DEPTH + length])
                ints_high[k, part, :length] = high
                ints_low[k, part, :length] = low
                if length < DEPTH:
                    nothing = jnp.zeros((16, DEPTH - length), BF16)
                    ints_high[k, part, length:] = nothing
                    ints_low[k, part, length:] = nothing
            return inner

        return lax.fori_loop(0, BLOCK // 16, split, carry)

    lax.fori_loop(0, blocks, split_block, 0)
    twin_copy.wait_recv()

    def near_step(j, carry):
        for p, total in ((0, even), (1, odd)):
            k = 2 * j + p
            parts = [
                mine[k], mine[slices + k], twin[k], twin[slices + k],
                mine[2 * slices + j], twin[2 * slices + j],
            ]
            total[...] += product(jnp.concatenate(parts, axis=0), k)
        return carry

    lax.fori_loop(0, slices // 2, near_step, 0)
    for s in range(2):
        for h in range(2):
            for g in range(2):
                at = 4 * third * s + 2 * third * g + third * h
                emit(s, h, g, even[at:at + third] + odd[at:at + third])
            at = 8 * third + 4 * small * s + small * h
            emit(s, h, 2, even[at:at + small] + odd[at + 2 * small:at + 3 * small])

    def arrive(i):
        far_copy(i).wait_recv()
        pass_copy(i).start()

    def far_block(i):
        pass_copy(i).wait_recv()
        return jnp.concatenate([far[i], far_twin[i]], axis=0)

    arrive(0)
    for g in range(2):
        group_sum[...] = jnp.zeros_like(group_sum)

        def far_step(k, carry):
            arrive(g * slices + k + 1)
            group_sum[...] += product(far_block(g * slices + k), k)
            return carry

        lax.fori_loop(0, slices, far_step, 0)
        for s in range(2):
            for h in range(2):
                at = 2 * third * s + third * h
                emit(2 + s, h, g, group_sum[at:at + third])

    last_even[...] = jnp.zeros_like(last_even)
    last_odd[...] = jnp.zeros_like(last_odd)

    def last_step(j, carry):
        @pl.when(j < slices // 2 - 1)
        def _():
            arrive(2 * slices + j + 1)

        block = far_block(2 * slices + j)
        last_even[...] += product(block, 2 * j)
        last_odd[...] += product(block, 2 * j + 1)
        return carry

    lax.fori_loop(0, slices // 2, last_step, 0)
    for s in range(2):
        for h in range(2):
            at = 4 * small * s + small * h
            emit(2 + s, h, 2, last_even[at:at + small] + last_odd[at + 2 * small:at + 3 * small])

    def drain(i, carry):
        far_copy(i).wait_send()
        pass_copy(i).wait_send()
        return carry

    lax.fori_loop(0, steps, drain, 0)
    twin_copy.wait_send()

    for g in range(3):
        for source in range(wides):
            @pl.when(me != source)
            def _():
                dst = recv_big.at[g, source] if g < 2 else recv_small.at[source]
                pltpu.make_async_remote_copy(
                    src_ref=dst, dst_ref=dst,
                    send_sem=sum_send.at[0, 0, g], recv_sem=sum_recv.at[g, source],
                    device_id=(source, narrow), device_id_type=MESH,
                ).wait_recv()
        held = recv_big.at[g] if g < 2 else recv_small
        total = held[0]
        for source in range(1, wides):
            total = total + held[source]
        out[g * third:g * third + total.shape[0], :] = total

    for s in range(4):
        for h in range(2):
            for g in range(3):
                owner, copy = sum_copy(s, h, g)

                @pl.when(owner != me)
                def _():
                    copy.wait_send()


def fused_term(amplitudes, integrals, wides):
    rows, pairs = amplitudes.shape
    cols = integrals.shape[1]
    owner_rows = rows // 2
    third = 2 * owner_rows // 5
    small = owner_rows - 2 * third
    slices = 2 * pl.cdiv(pairs, 2 * DEPTH)
    steps = 2 * slices + slices // 2
    chunks = pltpu.VMEM((steps, 2 * third, DEPTH), F32)
    near_rows = 8 * third + 8 * small
    far_rows = 4 * third
    dma = pltpu.SemaphoreType.DMA
    any_spec = pl.BlockSpec(memory_space=pl.ANY)
    return pl.pallas_call(
        functools.partial(cycle_kernel, wides),
        out_shape=jax.ShapeDtypeStruct((owner_rows, cols), F32),
        in_specs=[any_spec, any_spec],
        out_specs=pl.BlockSpec(memory_space=pltpu.VMEM),
        scratch_shapes=[
            pltpu.VMEM((rows, pairs), F32),
            chunks, chunks, chunks, chunks,
            pltpu.VMEM((cols, pairs), F32),
            pltpu.VMEM((slices, cols, DEPTH), BF16),
            pltpu.VMEM((slices, cols, DEPTH), BF16),
            pltpu.VMEM((near_rows, cols), F32),
            pltpu.VMEM((near_rows, cols), F32),
            pltpu.VMEM((far_rows, cols), F32),
            pltpu.VMEM((far_rows, cols), F32),
            pltpu.VMEM((far_rows, cols), F32),
            pltpu.VMEM((4, 2, 2, third, cols), F32),
            pltpu.VMEM((4, 2, small, cols), F32),
            pltpu.VMEM((2, wides, third, cols), F32),
            pltpu.VMEM((wides, small, cols), F32),
            dma, dma((cols // BLOCK,)), dma((steps,)), dma((steps,)), dma((steps,)), dma((steps,)),
            dma, dma, dma((4, 2, 3)), dma((3, wides)),
        ],
        compiler_params=pltpu.CompilerParams(
            collective_id=0, has_side_effects=True, vmem_limit_bytes=60 * 1024 * 1024
        ),
        cost_estimate=pl.CostEstimate(
            flops=6 * 4 * rows * pairs * cols,
            bytes_accessed=4 * pairs * (rows + cols),
            transcendentals=0,
        ),
    )(amplitudes, integrals.T)


def plain_term(amplitudes, integrals):
    partial_term = jnp.dot(
        lax.all_gather(amplitudes, "narrow", axis=0, tiled=True),
        integrals,
        precision=lax.Precision.HIGHEST,
        preferred_element_type=F32,
    )
    return lax.psum_scatter(partial_term, "wide", scatter_dimension=0, tiled=True)


def per_device(wides, narrows, amplitudes, integrals, occupied_energy, virtual_energy_rows, virtual_energy_cols):
    rows = amplitudes.shape[0]
    if narrows == 4 and wides == 8 and rows % 20 == 0 and integrals.shape[1] % BLOCK == 0:
        cycle_term = fused_term(amplitudes, integrals, wides)
    else:
        cycle_term = plain_term(amplitudes, integrals)
    row_count = cycle_term.shape[0]
    col_count = cycle_term.shape[1]
    row_first = lax.axis_index("wide") * row_count
    col_first = lax.axis_index("narrow") * col_count
    row_energy = (occupied_energy[None, :] - virtual_energy_rows[:, None]).reshape(-1)
    col_energy = (occupied_energy[None, :] - virtual_energy_cols[:, None]).reshape(-1)
    row_part = lax.dynamic_slice_in_dim(row_energy, row_first, row_count)
    col_part = lax.dynamic_slice_in_dim(col_energy, col_first, col_count)
    denominator = row_part[:, None] + col_part[None, :]
    return cycle_term / denominator


def solution(mesh):
    in_specs = (P("narrow", "wide"), P("wide", "narrow"), P(), P(), P())
    out_specs = P("wide", "narrow")
    body = functools.partial(per_device, mesh.shape["wide"], mesh.shape["narrow"])
    return jax.shard_map(
        body, mesh=mesh, in_specs=in_specs, out_specs=out_specs, check_vma=False
    )
```

profile of v0, /device:TPU:4, one launch (start us, length us, event | category | flops | bytes accessed | tf_op | source)
XLA Modules:
  0.0 68.9 jit_solution(14095068864776655579)
XLA Ops:
  0.0 0.7 %broadcast_subtract_fusion.1 = f32[4,60]{1,0:T(4,128)S(1)} fusion(f32[4]{0:T(128)} %param.8, f32[60]{0:T(128)} %param.7), kind=kLoop, calls=%fused_computation.2 | loop fusion | flops 240 | bytes 1216 | tf_op jit(solution)/shard_map/sub | solution.py:333
  0.7 0.1 sub.37
  0.8 0.1 dynamic_slice.6
  0.9 0.7 %broadcast_subtract_fusion = f32[32,60]{1,0:T(8,128)S(1)} fusion(f32[32]{0:T(128)} %param.9, f32[60]{0:T(128)} %param.7), kind=kLoop, calls=%fused_computation.1 | loop fusion | flops 1920 | bytes 8048 | tf_op jit(solution)/shard_map/sub | solution.py:334
  1.6 0.1 sub.41
  1.8 0.1 dynamic_slice.7
  1.8 65.5 %shard_map.55 = f32[30,480]{1,0:T(8,128)} custom-call(f32[60,9000]{1,0:T(8,128)} %amp.1, f32[480,9000]{1,0:T(8,128)} %bitcast.1), custom_call_target="tpu_custom_call" | custom-call | flops 6220800000 | bytes 19440000 | tf_op jit(solution)/shard_map/pallas_call | solution.py:279
  67.3 1.6 %add_divide_fusion = f32[30,480]{1,0:T(8,128)} fusion(f32[30,480]{1,0:T(8,128)} %shard_map.55, f32[480]{0:T(512)S(1)} %dynamic_slice.7, f32[30]{0:T(128)S(1)} %dynamic_slice.6), kind=kLoop, calls=%fused_computation | loop fusion | flops 28800 | bytes 117240 | tf_op jit(solution)/shard_map/div | solution.py:338
where the time goes:
time: 69 us; the launch traced here: 68.9 us
  Pallas kernels  65.5 us (95%)
  other arithmetic  3.04 us (4%)
    pallas_call x1, Pallas kernels, fused_term(): pl.pallas_call(functools.partial(cycle_kernel, wides), out_shape=jax.Shap...  65.5 us
    div x1, other arithmetic, per_device(): return cycle_term / denominator  1.55 us

commit v1 on v0

--- a/solution.py
+++ b/solution.py
@@ -11,6 +11,7 @@
 F32 = jnp.float32
 BF16 = jnp.bfloat16
 DEPTH = 1152
+AHEAD = 4
 BLOCK = 80
 
 
@@ -26,12 +27,13 @@
 
 
 def cycle_kernel(
-    wides, amp, ints, out,
+    wides, amp, ints, occupied, virtual_rows, virtual_cols, out,
     own, mine, twin, far, far_twin, wide_ints, ints_high, ints_low,
     even, odd, group_sum, last_even, last_odd,
     send_big, send_small, recv_big, recv_small,
     own_sem, ints_sem, far_send, far_recv, pass_send, pass_recv, twin_send, twin_recv,
     sum_send, sum_recv,
+    occupied_lanes, occupied_cells, rows_cells, cols_cells, col_part, bottom, energy_sem,
 ):
     rows, pairs = amp.shape
     owner_rows = rows // 2
@@ -55,6 +57,15 @@
         part = pl.ds(b * BLOCK, BLOCK)
         return pltpu.make_async_copy(ints.at[part], wide_ints.at[part], ints_sem.at[b])
 
+    energies = (
+        (occupied, occupied_lanes), (occupied, occupied_cells),
+        (virtual_rows, rows_cells), (virtual_cols, cols_cells),
+    )
+    energy_copies = [
+        pltpu.make_async_copy(src, dst, energy_sem.at[e]) for e, (src, dst) in enumerate(energies)
+    ]
+    for copy in energy_copies:
+        copy.start()
     blocks = ints.shape[0] // BLOCK
     for b in range(blocks):
         ints_copy(b).start()
@@ -99,14 +110,30 @@
             i = g * slices + k
             pack(i, 0, g * third, third, k)
             pack(i, third, owner_rows + g * third, third, k)
-            far_copy(i).start()
+            if i < AHEAD // 2:
+                far_copy(i).start()
     for j in range(slices // 2):
         i = 2 * slices + j
         for p in range(2):
             pack(i, 2 * small * p, 2 * third, small, 2 * j + p)
             pack(i, 2 * small * p + small, owner_rows + 2 * third, small, 2 * j + p)
+    twin_copy.start()
+    for i in range(AHEAD // 2, AHEAD):
         far_copy(i).start()
-    twin_copy.start()
+
+    occupied_count = occupied.shape[0]
+    for copy in energy_copies:
+        copy.wait()
+    for b in range(ints.shape[0] // occupied_count):
+        col_part[:, b * occupied_count:(b + 1) * occupied_count] = (
+            occupied_lanes[...].reshape(1, occupied_count)
+            - cols_cells[narrow * (ints.shape[0] // occupied_count) + b]
+        )
+    first = me * owner_rows
+    virtual = rows_cells[lax.div(first, occupied_count)]
+    for r in range(owner_rows):
+        row_part = occupied_cells[lax.rem(first, occupied_count) + r] - virtual
+        bottom[r:r + 1, :] = row_part + col_part[...]
 
     def sum_copy(s, h, g):
         owner = 2 * shards[s] + h
@@ -163,10 +190,19 @@
                     ints_low[k, part, length:] = nothing
             return inner
 
-        return lax.fori_loop(0, BLOCK // 16, split, carry)
+        lax.fori_loop(0, BLOCK // 16, split, 0)
+
+        @pl.when(lax.rem(b, 2) == 1)
+        def _():
+            far_copy(AHEAD + lax.div(b, 2)).start()
+
+        return carry
 
     lax.fori_loop(0, blocks, split_block, 0)
     twin_copy.wait_recv()
+
+    early = AHEAD + blocks // 2
+    issued = early + slices // 2
 
     def near_step(j, carry):
         for p, total in ((0, even), (1, odd)):
@@ -176,6 +212,7 @@
                 mine[2 * slices + j], twin[2 * slices + j],
             ]
             total[...] += product(jnp.concatenate(parts, axis=0), k)
+        far_copy(early + j).start()
         return carry
 
     lax.fori_loop(0, slices // 2, near_step, 0)
@@ -190,6 +227,10 @@
     def arrive(i):
         far_copy(i).wait_recv()
         pass_copy(i).start()
+
+        @pl.when((i >= issued - AHEAD) & (i < steps - AHEAD))
+        def _():
+            far_copy(i + AHEAD).start()
 
     def far_block(i):
         pass_copy(i).wait_recv()
@@ -251,7 +292,8 @@
         total = held[0]
         for source in range(1, wides):
             total = total + held[source]
-        out[g * third:g * third + total.shape[0], :] = total
+        part = pl.ds(g * third, total.shape[0])
+        out[part, :] = total / bottom[part, :]
 
     for s in range(4):
         for h in range(2):
@@ -263,7 +305,7 @@
                     copy.wait_send()
 
 
-def fused_term(amplitudes, integrals, wides):
+def fused_step(wides, amplitudes, integrals, occupied, virtual_rows, virtual_cols):
     rows, pairs = amplitudes.shape
     cols = integrals.shape[1]
     owner_rows = rows // 2
@@ -279,7 +321,7 @@
     return pl.pallas_call(
         functools.partial(cycle_kernel, wides),
         out_shape=jax.ShapeDtypeStruct((owner_rows, cols), F32),
-        in_specs=[any_spec, any_spec],
+        in_specs=[any_spec] * 5,
         out_specs=pl.BlockSpec(memory_space=pltpu.VMEM),
         scratch_shapes=[
             pltpu.VMEM((rows, pairs), F32),
@@ -298,6 +340,13 @@
             pltpu.VMEM((wides, small, cols), F32),
             dma, dma((cols // BLOCK,)), dma((steps,)), dma((steps,)), dma((steps,)), dma((steps,)),
             dma, dma, dma((4, 2, 3)), dma((3, wides)),
+            pltpu.VMEM(occupied.shape, F32),
+            pltpu.SMEM(occupied.shape, F32),
+            pltpu.SMEM(virtual_rows.shape, F32),
+            pltpu.SMEM(virtual_cols.shape, F32),
+            pltpu.VMEM((1, cols), F32),
+            pltpu.VMEM((owner_rows, cols), F32),
+            dma((4,)),
         ],
         compiler_params=pltpu.CompilerParams(
             collective_id=0, has_side_effects=True, vmem_limit_bytes=60 * 1024 * 1024
@@ -307,7 +356,7 @@
             bytes_accessed=4 * pairs * (rows + cols),
             transcendentals=0,
         ),
-    )(amplitudes, integrals.T)
+    )(amplitudes, integrals.T, occupied, virtual_rows, virtual_cols)
 
 
 def plain_term(amplitudes, integrals):
@@ -323,9 +372,11 @@
 def per_device(wides, narrows, amplitudes, integrals, occupied_energy, virtual_energy_rows, virtual_energy_cols):
     rows = amplitudes.shape[0]
     if narrows == 4 and wides == 8 and rows % 20 == 0 and integrals.shape[1] % BLOCK == 0:
-        cycle_term = fused_term(amplitudes, integrals, wides)
-    else:
-        cycle_term = plain_term(amplitudes, integrals)
+        return fused_step(
+            wides, amplitudes, integrals,
+            occupied_energy, virtual_energy_rows, virtual_energy_cols,
+        )
+    cycle_term = plain_term(amplitudes, integrals)
     row_count = cycle_term.shape[0]
     col_count = cycle_term.shape[1]
     row_first = lax.axis_index("wide") * row_count

time: 69 us -> 67.1 us (0.972)
  other arithmetic: 3.04 us -> 0 us
  local copies, waits for them, and re-layouts: 0.34 us -> 1.47 us
    div x1 -> x0, other arithmetic: 1.55 us -> none  [per_device(): return cycle_term / denominator]
    sub x2 -> x0, other arithmetic: 1.48 us -> none  [the longest x1 0.74 us: per_device(): occupied_energy[None, :] - virtual_energy_cols[:, None]]
    unnamed x0 -> x1, local copies, waits for them, and re-layouts: none -> 1.47 us
where the time goes in v1:
time: 67.1 us; the launch traced here: 67 us
  Pallas kernels  65.5 us (98%)
  local copies, waits for them, and re-layouts  1.47 us (2%)
    pallas_call x1, Pallas kernels, fused_step(): pl.pallas_call(functools.partial(cycle_kernel, wides), out_shape=jax.Shap...  65.5 us
    unnamed x1, local copies, waits for them, and re-layouts  1.47 us

profile of v1, /device:TPU:4, one launch (start us, length us, event | category | flops | bytes accessed | tf_op | source)
XLA Modules:
  0.0 67.0 jit_solution(8623397013123063244)
XLA Ops:
  0.0 65.5 %shard_map.55 = f32[30,480]{1,0:T(8,128)} custom-call(f32[60,9000]{1,0:T(8,128)} %amp.1, f32[480,9000]{1,0:T(8,128)} %bitcast.1, f32[60]{0:T(128)} %occupied.1, f32[4]{0:T(128)} %virtual_rows.1, f32[32]{0:T(128)} %virtual_cols.1), custom_call_target="tpu_custom_call" | custom-call | flops 6220800000 | bytes 19440000 | tf_op jit(solution)/shard_map/pallas_call | solution.py:321
  65.5 1.5 %copy.7 = f32[30,480]{1,0:T(8,128)} copy(f32[30,480]{1,0:T(8,128)} %shard_map.55) | data formatting | bytes 115200

commit v2 on v1

--- a/solution.py
+++ b/solution.py
@@ -29,7 +29,7 @@
 def cycle_kernel(
     wides, amp, ints, occupied, virtual_rows, virtual_cols, out,
     own, mine, twin, far, far_twin, wide_ints, ints_high, ints_low,
-    even, odd, group_sum, last_even, last_odd,
+    even, odd, group_sum, far_even, far_odd,
     send_big, send_small, recv_big, recv_small,
     own_sem, ints_sem, far_send, far_recv, pass_send, pass_recv, twin_send, twin_recv,
     sum_send, sum_recv,
@@ -41,6 +41,9 @@
     small = owner_rows - 2 * third
     steps = mine.shape[0]
     slices = ints_high.shape[0]
+    last_length = pl.cdiv(pairs - (slices - 1) * DEPTH, 128) * 128
+    first_length = pl.cdiv(last_length, 256) * 128
+    light = 3 * slices // 2
     me = lax.axis_index("wide")
     narrow = lax.axis_index("narrow")
     across = lax.div(narrow, 2)
@@ -67,8 +70,6 @@
     for copy in energy_copies:
         copy.start()
     blocks = ints.shape[0] // BLOCK
-    for b in range(blocks):
-        ints_copy(b).start()
 
     barrier = pltpu.get_barrier_semaphore()
     for other in (sibling, neighbour):
@@ -79,17 +80,26 @@
         )
     pl.semaphore_wait(barrier, wides + 1)
 
-    def far_copy(i):
+    last_part = [(0, first_length), (first_length, last_length - first_length)]
+
+    def chunk(buffer, i, piece):
+        if piece is None:
+            return buffer.at[i]
+        return buffer.at[i, :, pl.ds(*last_part[piece])]
+
+    def far_copy(i, piece=None):
+        at = i + (piece or 0)
         return pltpu.make_async_remote_copy(
-            src_ref=mine.at[i], dst_ref=far.at[i],
-            send_sem=far_send.at[i], recv_sem=far_recv.at[i],
+            src_ref=chunk(mine, i, piece), dst_ref=chunk(far, i, piece),
+            send_sem=far_send.at[at], recv_sem=far_recv.at[at],
             device_id=(me, neighbour), device_id_type=MESH,
         )
 
-    def pass_copy(i):
+    def pass_copy(i, piece=None):
+        at = i + (piece or 0)
         return pltpu.make_async_remote_copy(
-            src_ref=far.at[i], dst_ref=far_twin.at[i],
-            send_sem=pass_send.at[i], recv_sem=pass_recv.at[i],
+            src_ref=chunk(far, i, piece), dst_ref=chunk(far_twin, i, piece),
+            send_sem=pass_send.at[at], recv_sem=pass_recv.at[at],
             device_id=(me, sibling), device_id_type=MESH,
         )
 
@@ -105,18 +115,22 @@
             mine[i, at:at + count, length:] = jnp.zeros((count, DEPTH - length), F32)
 
     own_copy.wait()
-    for g in range(2):
-        for k in range(slices):
-            i = g * slices + k
-            pack(i, 0, g * third, third, k)
-            pack(i, third, owner_rows + g * third, third, k)
-            if i < AHEAD // 2:
+    for j in range(slices // 2):
+        for p in range(2):
+            pack(3 * j, 2 * small * p, 2 * third, small, 2 * j + p)
+            pack(3 * j, 2 * small * p + small, owner_rows + 2 * third, small, 2 * j + p)
+        for p in range(2):
+            i = 3 * j + 1 + p
+            pack(i, 0, 0, third, 2 * j + p)
+            pack(i, third, owner_rows, third, 2 * j + p)
+        if j == 0:
+            for i in range(AHEAD // 2):
                 far_copy(i).start()
-    for j in range(slices // 2):
-        i = 2 * slices + j
-        for p in range(2):
-            pack(i, 2 * small * p, 2 * third, small, 2 * j + p)
-            pack(i, 2 * small * p + small, owner_rows + 2 * third, small, 2 * j + p)
+            for b in range(blocks):
+                ints_copy(b).start()
+    for k in range(slices):
+        pack(light + k, 0, third, third, k)
+        pack(light + k, third, owner_rows + third, third, k)
     twin_copy.start()
     for i in range(AHEAD // 2, AHEAD):
         far_copy(i).start()
@@ -164,11 +178,11 @@
         def _():
             copy.start()
 
-    def product(values, k):
+    def product(values, k, part=(0, DEPTH)):
         high, low = halves(values)
         count = values.shape[0]
-        both = by_rows(jnp.concatenate([high, low], axis=0), ints_high[k])
-        rest = by_rows(high, ints_low[k])
+        both = by_rows(jnp.concatenate([high, low], axis=0), ints_high[k, :, pl.ds(*part)])
+        rest = by_rows(high, ints_low[k, :, pl.ds(*part)])
         return both[:count] + (both[count:] + rest)
 
     even[...] = jnp.zeros_like(even)
@@ -208,8 +222,8 @@
         for p, total in ((0, even), (1, odd)):
             k = 2 * j + p
             parts = [
-                mine[k], mine[slices + k], twin[k], twin[slices + k],
-                mine[2 * slices + j], twin[2 * slices + j],
+                mine[3 * j + 1 + p], mine[light + k], twin[3 * j + 1 + p], twin[light + k],
+                mine[3 * j], twin[3 * j],
             ]
             total[...] += product(jnp.concatenate(parts, axis=0), k)
         far_copy(early + j).start()
@@ -228,54 +242,86 @@
         far_copy(i).wait_recv()
         pass_copy(i).start()
 
-        @pl.when((i >= issued - AHEAD) & (i < steps - AHEAD))
+        @pl.when((i >= issued - AHEAD) & (i < steps - 1 - AHEAD))
         def _():
             far_copy(i + AHEAD).start()
 
-    def far_block(i):
-        pass_copy(i).wait_recv()
-        return jnp.concatenate([far[i], far_twin[i]], axis=0)
-
+        @pl.when(i == steps - 1 - AHEAD)
+        def _():
+            for piece in range(2):
+                far_copy(steps - 1, piece).start()
+
+    def arrive_last(piece):
+        far_copy(steps - 1, piece).wait_recv()
+        pass_copy(steps - 1, piece).start()
+
+    far_even[...] = jnp.zeros_like(far_even)
+    far_odd[...] = jnp.zeros_like(far_odd)
     arrive(0)
-    for g in range(2):
-        group_sum[...] = jnp.zeros_like(group_sum)
-
-        def far_step(k, carry):
-            arrive(g * slices + k + 1)
-            group_sum[...] += product(far_block(g * slices + k), k)
-            return carry
-
-        lax.fori_loop(0, slices, far_step, 0)
-        for s in range(2):
-            for h in range(2):
-                at = 2 * third * s + third * h
-                emit(2 + s, h, g, group_sum[at:at + third])
-
-    last_even[...] = jnp.zeros_like(last_even)
-    last_odd[...] = jnp.zeros_like(last_odd)
-
-    def last_step(j, carry):
+    arrive(1)
+
+    def far_step(j, carry):
+        arrive(3 * j + 2)
+        pass_copy(3 * j).wait_recv()
+        pass_copy(3 * j + 1).wait_recv()
+        parts = [far[3 * j + 1], far_twin[3 * j + 1], far[3 * j], far_twin[3 * j]]
+        far_even[...] += product(jnp.concatenate(parts, axis=0), 2 * j)
+        arrive(3 * j + 3)
+
         @pl.when(j < slices // 2 - 1)
         def _():
-            arrive(2 * slices + j + 1)
-
-        block = far_block(2 * slices + j)
-        last_even[...] += product(block, 2 * j)
-        last_odd[...] += product(block, 2 * j + 1)
+            arrive(3 * j + 4)
+
+        pass_copy(3 * j + 2).wait_recv()
+        parts = [far[3 * j + 2], far_twin[3 * j + 2], far[3 * j], far_twin[3 * j]]
+        far_odd[...] += product(jnp.concatenate(parts, axis=0), 2 * j + 1)
         return carry
 
-    lax.fori_loop(0, slices // 2, last_step, 0)
+    lax.fori_loop(0, slices // 2, far_step, 0)
     for s in range(2):
         for h in range(2):
-            at = 4 * small * s + small * h
-            emit(2 + s, h, 2, last_even[at:at + small] + last_odd[at + 2 * small:at + 3 * small])
+            at = 2 * third * s + third * h
+            emit(2 + s, h, 0, far_even[at:at + third] + far_odd[at:at + third])
+            at = 4 * third + 4 * small * s + small * h
+            emit(2 + s, h, 2, far_even[at:at + small] + far_odd[at + 2 * small:at + 3 * small])
+
+    def light_product(k):
+        pass_copy(light + k).wait_recv()
+        group_sum[...] += product(
+            jnp.concatenate([far[light + k], far_twin[light + k]], axis=0), k
+        )
+
+    def light_step(k, carry):
+        arrive(light + k + 1)
+        light_product(k)
+        return carry
+
+    group_sum[...] = jnp.zeros_like(group_sum)
+    lax.fori_loop(0, slices - 2, light_step, 0)
+    arrive_last(0)
+    light_product(slices - 2)
+    arrive_last(1)
+    for piece in range(2):
+        pass_copy(steps - 1, piece).wait_recv()
+        part = pl.ds(*last_part[piece])
+        group_sum[...] += product(
+            jnp.concatenate([far[steps - 1, :, part], far_twin[steps - 1, :, part]], axis=0),
+            slices - 1, last_part[piece],
+        )
+    for s in range(2):
+        for h in range(2):
+            at = 2 * third * s + third * h
+            emit(2 + s, h, 1, group_sum[at:at + third])
 
     def drain(i, carry):
         far_copy(i).wait_send()
         pass_copy(i).wait_send()
         return carry
 
-    lax.fori_loop(0, steps, drain, 0)
+    lax.fori_loop(0, steps - 1, drain, 0)
+    for piece in range(2):
+        far_copy(steps - 1, piece).wait_send()
+        pass_copy(steps - 1, piece).wait_send()
     twin_copy.wait_send()
 
     for g in range(3):
@@ -332,13 +378,14 @@
             pltpu.VMEM((near_rows, cols), F32),
             pltpu.VMEM((near_rows, cols), F32),
             pltpu.VMEM((far_rows, cols), F32),
-            pltpu.VMEM((far_rows, cols), F32),
-            pltpu.VMEM((far_rows, cols), F32),
+            pltpu.VMEM((far_rows + 8 * small, cols), F32),
+            pltpu.VMEM((far_rows + 8 * small, cols), F32),
             pltpu.VMEM((4, 2, 2, third, cols), F32),
             pltpu.VMEM((4, 2, small, cols), F32),
             pltpu.VMEM((2, wides, third, cols), F32),
             pltpu.VMEM((wides, small, cols), F32),
-            dma, dma((cols // BLOCK,)), dma((steps,)), dma((steps,)), dma((steps,)), dma((steps,)),
+            dma, dma((cols // BLOCK,)), dma((steps + 1,)), dma((steps + 1,)),
+            dma((steps + 1,)), dma((steps + 1,)),
             dma, dma, dma((4, 2, 3)), dma((3, wides)),
             pltpu.VMEM(occupied.shape, F32),
             pltpu.SMEM(occupied.shape, F32),

time: 67.1 us -> 65.2 us (0.972); the launches traced: 67 us -> 64 us
  Pallas kernels: 65.5 us -> 62.5 us
    pallas_call x1, Pallas kernels: 65.5 us -> 62.5 us  [fused_step(): pl.pallas_call(functools.partial(cycle_kernel, wides), out_shape=jax.Shap...]
where the time goes in v2:
time: 65.2 us; the launch traced here: 64 us
  Pallas kernels  62.5 us (96%)
  local copies, waits for them, and re-layouts  1.47 us (2%)
    pallas_call x1, Pallas kernels, fused_step(): pl.pallas_call(functools.partial(cycle_kernel, wides), out_shape=jax.Shap...  62.5 us
    unnamed x1, local copies, waits for them, and re-layouts  1.47 us

profile of v2, /device:TPU:4, one launch (start us, length us, event | category | flops | bytes accessed | tf_op | source)
XLA Modules:
  0.0 64.0 jit_solution(17876181933050051468)
XLA Ops:
  0.0 62.5 %shard_map.55 = f32[30,480]{1,0:T(8,128)} custom-call(f32[60,9000]{1,0:T(8,128)} %amp.1, f32[480,9000]{1,0:T(8,128)} %bitcast.1, f32[60]{0:T(128)} %occupied.1, f32[4]{0:T(128)} %virtual_rows.1, f32[32]{0:T(128)} %virtual_cols.1), custom_call_target="tpu_custom_call" | custom-call | flops 6220800000 | bytes 19440000 | tf_op jit(solution)/shard_map/pallas_call | solution.py:367
  62.5 1.5 %copy.7 = f32[30,480]{1,0:T(8,128)} copy(f32[30,480]{1,0:T(8,128)} %shard_map.55) | data formatting | bytes 115200

commit v3 on v2

--- a/solution.py
+++ b/solution.py
@@ -33,7 +33,7 @@
     send_big, send_small, recv_big, recv_small,
     own_sem, ints_sem, far_send, far_recv, pass_send, pass_recv, twin_send, twin_recv,
     sum_send, sum_recv,
-    occupied_lanes, occupied_cells, rows_cells, cols_cells, col_part, bottom, energy_sem,
+    occupied_lanes, occupied_cells, rows_cells, cols_cells, col_part, bottom, energy_sem, result, out_sem,
 ):
     rows, pairs = amp.shape
     owner_rows = rows // 2
@@ -216,7 +216,7 @@
     twin_copy.wait_recv()
 
     early = AHEAD + blocks // 2
-    issued = early + slices // 2
+    issued = early + slices
 
     def near_step(j, carry):
         for p, total in ((0, even), (1, odd)):
@@ -226,7 +226,8 @@
                 mine[3 * j], twin[3 * j],
             ]
             total[...] += product(jnp.concatenate(parts, axis=0), k)
-        far_copy(early + j).start()
+        for p in range(2):
+            far_copy(early + 2 * j + p).start()
         return carry
 
     lax.fori_loop(0, slices // 2, near_step, 0)
@@ -324,7 +325,7 @@
         pass_copy(steps - 1, piece).wait_send()
     twin_copy.wait_send()
 
-    for g in range(3):
+    for g in (0, 2, 1):
         for source in range(wides):
             @pl.when(me != source)
             def _():
@@ -339,8 +340,10 @@
         for source in range(1, wides):
             total = total + held[source]
         part = pl.ds(g * third, total.shape[0])
-        out[part, :] = total / bottom[part, :]
-
+        result[part, :] = total / bottom[part, :]
+
+    out_copy = pltpu.make_async_copy(result, out, out_sem)
+    out_copy.start()
     for s in range(4):
         for h in range(2):
             for g in range(3):
@@ -349,6 +352,7 @@
                 @pl.when(owner != me)
                 def _():
                     copy.wait_send()
+    out_copy.wait()
 
 
 def fused_step(wides, amplitudes, integrals, occupied, virtual_rows, virtual_cols):
@@ -364,11 +368,12 @@
     far_rows = 4 * third
     dma = pltpu.SemaphoreType.DMA
     any_spec = pl.BlockSpec(memory_space=pl.ANY)
+    hbm_spec = pl.BlockSpec(memory_space=pltpu.HBM)
     return pl.pallas_call(
         functools.partial(cycle_kernel, wides),
         out_shape=jax.ShapeDtypeStruct((owner_rows, cols), F32),
-        in_specs=[any_spec] * 5,
-        out_specs=pl.BlockSpec(memory_space=pltpu.VMEM),
+        in_specs=[hbm_spec] * 5,
+        out_specs=any_spec,
         scratch_shapes=[
             pltpu.VMEM((rows, pairs), F32),
             chunks, chunks, chunks, chunks,
@@ -394,9 +399,10 @@
             pltpu.VMEM((1, cols), F32),
             pltpu.VMEM((owner_rows, cols), F32),
             dma((4,)),
+            pltpu.VMEM((owner_rows, cols), F32), dma,
         ],
         compiler_params=pltpu.CompilerParams(
-            collective_id=0, has_side_effects=True, vmem_limit_bytes=60 * 1024 * 1024
+            collective_id=0, has_side_effects=True, vmem_limit_bytes=52 * 1024 * 1024
         ),
         cost_estimate=pl.CostEstimate(
             flops=6 * 4 * rows * pairs * cols,

time: 65.2 us -> 65.7 us (level)
  local copies, waits for them, and re-layouts: 1.47 us -> 2.6 us
    unnamed x1 -> x7, local copies, waits for them, and re-layouts: 1.47 us -> 2.6 us
where the time goes in v3:
time: 65.7 us; the launch traced here: 64.6 us
  Pallas kernels  61.9 us (94%)
  local copies, waits for them, and re-layouts  2.6 us (4%)
    pallas_call x1, Pallas kernels, fused_step(): pl.pallas_call(functools.partial(cycle_kernel, wides), out_shape=jax.Shap...  61.9 us
    unnamed x7, local copies, waits for them, and re-layouts  2.6 us

profile of v3, /device:TPU:4, one launch (start us, length us, event | category | flops | bytes accessed | tf_op | source)
XLA Modules:
  0.0 64.6 jit_solution(15468432954405137684)
XLA Ops:
  0.0 0.0 copy-start
  0.0 0.7 %copy-done = f32[60]{0:T(128)S(1)} copy-done((f32[60]{0:T(128)S(1)}, f32[60]{0:T(128)}, u32[]{:S(2)}) %copy-start) | copy-done | bytes 264
  0.7 0.0 copy-start.1
  0.7 0.7 %copy-done.1 = f32[4]{0:T(128)S(1)} copy-done((f32[4]{0:T(128)S(1)}, f32[4]{0:T(128)}, u32[]{:S(2)}) %copy-start.1) | copy-done | bytes 40
  1.3 0.0 copy-start.2
  1.3 0.7 %copy-done.2 = f32[32]{0:T(128)S(1)} copy-done((f32[32]{0:T(128)S(1)}, f32[32]{0:T(128)}, u32[]{:S(2)}) %copy-start.2) | copy-done | bytes 152
  2.0 61.9 %shard_map.55 = f32[30,480]{1,0:T(8,128)S(1)} custom-call(f32[60,9000]{1,0:T(8,128)} %amp.1, f32[480,9000]{1,0:T(8,128)} %bitcast.1, f32[60]{0:T(128)S(1)} %copy-done, f32[4]{0:T(128)S(1)} %copy-done.1, f32[32]{0:T(128)S(1)} %copy-done.2), custom_call_target="tpu_custom_call" | custom-call | flops 6220800000 | bytes 19440000 | tf_op jit(solution)/shard_map/pallas_call | solution.py:372
  63.9 0.6 copy.7
Async XLA Ops:
  0.0 0.7 %copy-start = (f32[60]{0:T(128)S(1)}, f32[60]{0:T(128)}, u32[]{:S(2)}) copy-start(f32[60]{0:T(128)} %occupied.1) | copy-start | bytes 724
  0.7 0.7 %copy-start.1 = (f32[4]{0:T(128)S(1)}, f32[4]{0:T(128)}, u32[]{:S(2)}) copy-start(f32[4]{0:T(128)} %virtual_rows.1) | copy-start | bytes 52
  1.3 0.7 %copy-start.2 = (f32[32]{0:T(128)S(1)}, f32[32]{0:T(128)}, u32[]{:S(2)}) copy-start(f32[32]{0:T(128)} %virtual_cols.1) | copy-start | bytes 388

commit v4 on v3

--- a/solution.py
+++ b/solution.py
@@ -27,13 +27,13 @@
 
 
 def cycle_kernel(
-    wides, amp, ints, occupied, virtual_rows, virtual_cols, out,
+    wides, occupied_count, rows_count, amp, ints, cells, out,
     own, mine, twin, far, far_twin, wide_ints, ints_high, ints_low,
     even, odd, group_sum, far_even, far_odd,
     send_big, send_small, recv_big, recv_small,
     own_sem, ints_sem, far_send, far_recv, pass_send, pass_recv, twin_send, twin_recv,
     sum_send, sum_recv,
-    occupied_lanes, occupied_cells, rows_cells, cols_cells, col_part, bottom, energy_sem, result, out_sem,
+    col_part, bottom, result, out_sem,
 ):
     rows, pairs = amp.shape
     owner_rows = rows // 2
@@ -60,15 +60,6 @@
         part = pl.ds(b * BLOCK, BLOCK)
         return pltpu.make_async_copy(ints.at[part], wide_ints.at[part], ints_sem.at[b])
 
-    energies = (
-        (occupied, occupied_lanes), (occupied, occupied_cells),
-        (virtual_rows, rows_cells), (virtual_cols, cols_cells),
-    )
-    energy_copies = [
-        pltpu.make_async_copy(src, dst, energy_sem.at[e]) for e, (src, dst) in enumerate(energies)
-    ]
-    for copy in energy_copies:
-        copy.start()
     blocks = ints.shape[0] // BLOCK
 
     barrier = pltpu.get_barrier_semaphore()
@@ -135,18 +126,20 @@
     for i in range(AHEAD // 2, AHEAD):
         far_copy(i).start()
 
-    occupied_count = occupied.shape[0]
-    for copy in energy_copies:
-        copy.wait()
+    cols_at = occupied_count + rows_count
+    lane = lax.broadcasted_iota(jnp.int32, (1, occupied_count), 1)
+    occupied_lanes = jnp.zeros((1, occupied_count), F32)
+    for i in range(occupied_count):
+        occupied_lanes = jnp.where(lane == i, cells[i], occupied_lanes)
     for b in range(ints.shape[0] // occupied_count):
         col_part[:, b * occupied_count:(b + 1) * occupied_count] = (
-            occupied_lanes[...].reshape(1, occupied_count)
-            - cols_cells[narrow * (ints.shape[0] // occupied_count) + b]
+            occupied_lanes
+            - cells[cols_at + narrow * (ints.shape[0] // occupied_count) + b]
         )
     first = me * owner_rows
-    virtual = rows_cells[lax.div(first, occupied_count)]
+    virtual = cells[occupied_count + lax.div(first, occupied_count)]
     for r in range(owner_rows):
-        row_part = occupied_cells[lax.rem(first, occupied_count) + r] - virtual
+        row_part = cells[lax.rem(first, occupied_count) + r] - virtual
         bottom[r:r + 1, :] = row_part + col_part[...]
 
     def sum_copy(s, h, g):
@@ -368,11 +361,11 @@
     far_rows = 4 * third
     dma = pltpu.SemaphoreType.DMA
     any_spec = pl.BlockSpec(memory_space=pl.ANY)
-    hbm_spec = pl.BlockSpec(memory_space=pltpu.HBM)
+    cell_spec = pl.BlockSpec(memory_space=pltpu.SMEM)
     return pl.pallas_call(
-        functools.partial(cycle_kernel, wides),
+        functools.partial(cycle_kernel, wides, occupied.shape[0], virtual_rows.shape[0]),
         out_shape=jax.ShapeDtypeStruct((owner_rows, cols), F32),
-        in_specs=[hbm_spec] * 5,
+        in_specs=[any_spec, any_spec, cell_spec],
         out_specs=any_spec,
         scratch_shapes=[
             pltpu.VMEM((rows, pairs), F32),
@@ -392,13 +385,8 @@
             dma, dma((cols // BLOCK,)), dma((steps + 1,)), dma((steps + 1,)),
             dma((steps + 1,)), dma((steps + 1,)),
             dma, dma, dma((4, 2, 3)), dma((3, wides)),
-            pltpu.VMEM(occupied.shape, F32),
-            pltpu.SMEM(occupied.shape, F32),
-            pltpu.SMEM(virtual_rows.shape, F32),
-            pltpu.SMEM(virtual_cols.shape, F32),
             pltpu.VMEM((1, cols), F32),
             pltpu.VMEM((owner_rows, cols), F32),
-            dma((4,)),
             pltpu.VMEM((owner_rows, cols), F32), dma,
         ],
         compiler_params=pltpu.CompilerParams(
@@ -409,7 +397,7 @@
             bytes_accessed=4 * pairs * (rows + cols),
             transcendentals=0,
         ),
-    )(amplitudes, integrals.T, occupied, virtual_rows, virtual_cols)
+    )(amplitudes, integrals.T, jnp.concatenate([occupied, virtual_rows, virtual_cols]))
 
 
 def plain_term(amplitudes, integrals):

time: 65.7 us -> 65.1 us (level)
  local copies, waits for them, and re-layouts: 2.6 us -> 0.63 us
  other arithmetic: 0 us -> 0.76 us
    unnamed x7 -> x1, local copies, waits for them, and re-layouts: 2.6 us -> 0.63 us
    concatenate x0 -> x1, other arithmetic: none -> 0.76 us  [fused_step(): jnp.concatenate([occupied, virtual_rows, virtual_cols])]
where the time goes in v4:
time: 65.1 us; the launch traced here: 63.9 us
  Pallas kernels  62.5 us (96%)
  other arithmetic  0.76 us (1%)
    pallas_call x1, Pallas kernels, fused_step(): pl.pallas_call(functools.partial(cycle_kernel, wides, occupied.shape[0],...  62.5 us

profile of v4, /device:TPU:4, one launch (start us, length us, event | category | flops | bytes accessed | tf_op | source)
XLA Modules:
  0.0 63.9 jit_solution(13275035774258210281)
XLA Ops:
  0.0 0.8 %pad_maximum_fusion.cells = f32[96]{0:T(128)S(1)} fusion(f32[32]{0:T(128)} %param.9, f32[4]{0:T(128)} %param.8, f32[60]{0:T(128)} %param.7), kind=kLoop, calls=%fused_computation | loop fusion | flops 192 | bytes 768 | tf_op jit(solution)/shard_map/concatenate | solution.py:400
  0.8 62.5 %shard_map.55 = f32[30,480]{1,0:T(8,128)S(1)} custom-call(f32[60,9000]{1,0:T(8,128)} %amp.1, f32[480,9000]{1,0:T(8,128)} %bitcast.1, f32[96]{0:T(128)S(1)} %pad_maximum_fusion.cells), custom_call_target="tpu_custom_call" | custom-call | flops 6220800000 | bytes 19440000 | tf_op jit(solution)/shard_map/pallas_call | solution.py:365
  63.2 0.6 copy.7
